TPU v7x, 512 devices: a whole 4x8x8 slice. The times are simulated.
512 devices in a mesh: vocab: 32 (over x, z), dp: 16 (over y, core).
Axes of the slice: x: 4, y: 8, z: 8, core: 2. Of those that a mesh axis runs over, the one named last changes fastest.
Arguments:
- out_grads: float32 [65536, 4096], P(('vocab', 'dp')), may hold values from -6 to 6
- token_ids: int32 [65536], P(('vocab', 'dp')), may hold values from 0 to 128255, as said below
Outputs:
- table_grad: bfloat16 [128256, 4096], P('vocab', 'dp')
Inputs may be any that keep to these rules, and one draw needn't show every extreme that they name: `token_ids`: call ids k * 4008 to (k + 1) * 4008 - 1 block k. The 128 tokens of one device hold at most 12 ids of any one block; one block, the same for all devices, holds exactly 12 ids of every device.
All inputs are finite; a program needn't handle non-finite values.
Results may differ from a plain program's by a relative error of at most 0.001.
Values sent between devices are 32-bit elements; how exact they have to be, the bound alone decides.
No kernel may reach another device: no remote copies, remote signals or barrier semaphores. Data moves between devices by JAX's collectives and lax.ppermute only.
A program may use at most 64 MiB of HBM per device.

v0:
```python
import jax
import jax.numpy as jnp
from jax import lax
from jax.sharding import PartitionSpec as P

VOCAB = 128256


def turned_gather(arrays, axis, dims):
    turned = [jnp.moveaxis(a, dim, 0) for a, dim in zip(arrays, dims)]
    both = jnp.concatenate([t.reshape(len(t), -1) for t in turned], axis=1)
    whole, at, outs = (lax.all_gather(both, axis, axis=0, tiled=True), 0, [])
    for t, dim in zip(turned, dims):
        share = whole[:, at : at + t[0].size].reshape(-1, *t.shape[1:])
        outs.append(jnp.moveaxis(share, 0, dim))
        at += t[0].size
    return tuple(outs)


def slot_tables(token_ids, rows_own, owners, capacity):
    tok_count = token_ids.shape[0]
    owner_of = token_ids // rows_own
    local_row = token_ids - owner_of * rows_own
    positions = lax.iota(jnp.int32, tok_count)
    earlier = (owner_of[:, None] == owner_of[None, :]) & (positions[None, :] < positions[:, None])
    slot_of = jnp.sum(earlier.astype(jnp.int32), axis=1)
    owner_ids = lax.iota(jnp.int32, owners)
    slot_ids = lax.iota(jnp.int32, capacity)
    matches = (owner_of[None, None, :] == owner_ids[:, None, None]) & (
        slot_of[None, None, :] == slot_ids[None, :, None]
    )
    filled = jnp.any(matches, axis=2)
    token_at = jnp.where(
        filled, jnp.sum(jnp.where(matches, positions[None, None, :], 0), axis=2), -1
    )
    row_at = jnp.where(filled, jnp.sum(jnp.where(matches, local_row[None, None, :], 0), axis=2), 0)
    return (token_at, row_at)


def local(out_grads, token_ids):
    owners = lax.axis_size("vocab")
    tok_count = token_ids.shape[0]
    rows_own = VOCAB // owners
    capacity = 3 * tok_count // owners
    token_at, row_at = slot_tables(token_ids, rows_own, owners, capacity)
    token_cols = lax.all_to_all(out_grads, "dp", split_axis=1, concat_axis=0, tiled=True)
    token_all, row_all = turned_gather((token_at, row_at), "dp", (1, 1))
    source = lax.broadcasted_iota(jnp.int32, token_all.shape, 1) // capacity
    index = source * tok_count + jnp.maximum(token_all, 0)
    picked = jnp.take(token_cols, index, axis=0)
    outgoing = jnp.where((token_all >= 0)[:, :, None], picked, 0.0)
    arrived, arrived_rows = (
        lax.all_to_all(outgoing, "vocab", split_axis=0, concat_axis=0, tiled=True),
        lax.all_to_all(row_all, "vocab", split_axis=0, concat_axis=0, tiled=True),
    )
    columns = arrived.reshape(-1, arrived.shape[2])
    row_index = arrived_rows.reshape(-1)
    table_sum = jax.ops.segment_sum(columns, row_index, num_segments=rows_own)
    return table_sum.astype(jnp.bfloat16)


def solution(mesh):
    in_specs = (P(("vocab", "dp"), None), P(("vocab", "dp")))
    out_specs = P("vocab", "dp")
    return jax.shard_map(local, mesh=mesh, in_specs=in_specs, out_specs=out_specs, check_vma=False)
```

profile of v0, /device:TPU:64, one launch (start us, length us, event | category | flops | bytes accessed | tf_op | source)
XLA Modules:
  0.0 306.3 jit_solution(15994949229476449633)
XLA Ops:
  0.0 0.0 copy-start
  0.0 3.2 %copy.28 = f32[16,16,8,256]{3,2,0,1:T(8,128)} copy(f32[16,16,8,256]{3,2,1,0:T(8,128)} %bitcast.29) | data formatting | bytes 4194304 | tf_op jit(solution)/shard_map/all_to_all | solution.py:46
  3.2 7.2 %all-to-all-start.1 = ((f32[128,16,256]{2,0,1:T(8,128)}), f32[128,16,256]{2,0,1:T(8,128)S(1)}, u32[]{:S(2)}, u32[]{:S(2)}) async-start(f32[128,16,256]{2,0,1:T(8,128)} %bitcast.28), calls=%async_computation.1 | async-start | bytes 4194304 | tf_op jit(solution)/shard_map/all_to_all | solution.py:46
  10.4 0.0 copy-done
  10.4 0.2 convert_reduce_fusion
  10.6 0.3 and_reduce_fusion
  10.9 0.5 fusion.2
  11.4 0.1 add_bitcast_fusion
  11.5 58.8 %all-gather = s32[16,12,64]{2,1,0:T(8,128)S(1)} all-gather(s32[1,12,64]{2,1,0:T(8,128)S(1)} %add_bitcast_fusion), channel_id=1, replica_groups=mesh['vocab'=32,'dp'=16] {'dp'}, dimensions={0}, use_global_device_ids=true | all-gather | bytes 52224 | tf_op jit(solution)/shard_map/all_gather | solution.py:12
  70.3 0.1 fusion.5
  70.4 0.1 copy.25
  70.5 0.1 reshape.67
  70.6 0.7 copy.22
  71.3 0.0 all-to-all-done.1
  71.3 12.6 %all-to-all-start = ((s32[32,1,192]{2,1,0:T(1,128)}), s32[32,1,192]{2,1,0:T(1,128)S(1)}, u32[]{:S(2)}, u32[]{:S(2)}) async-start(s32[32,1,192]{2,1,0:T(1,128)} %copy.22), calls=%async_computation | async-start | bytes 65536 | tf_op jit(solution)/shard_map/all_to_all | solution.py:54
  83.9 23.7 %gather_fusion = f32[6144,256]{1,0:T(8,128)} fusion(f32[2048,256]{1,0:T(8,128)S(1)} %bitcast.26, s32[6144]{0:T(1024)S(1)} %broadcast_clamp_fusion), kind=kCustom, calls=%fused_computation | custom fusion | bytes 12607488 | tf_op jit(solution)/shard_map/jit(_take)/gather | solution.py:50
  107.7 8.6 %select_select_fusion = f32[32,192,256]{2,1,0:T(8,128)} fusion(f32[32,192,256]{2,1,0:T(8,128)} %bitcast.27, pred[32,192]{1,0:T(8,128)(4,1)S(1)} %get-tuple-element.7, pred[32,192]{1,0:T(8,128)(4,1)S(1)} %compare_bitcast_fusion), kind=kLoop, calls=%fused_computation.2 | loop fusion | flops 3145728 | bytes 12595200 | tf_op jit(solution)/shard_map/jit(_where)/select_n | solution.py:51
  116.3 0.0 all-to-all-done
  116.3 9.8 %all-to-all-start.2 = ((f32[32,192,256]{2,1,0:T(8,128)}), f32[32,192,256]{2,1,0:T(8,128)}, u32[]{:S(2)}, u32[]{:S(2)}) async-start(f32[32,192,256]{2,1,0:T(8,128)} %select_select_fusion), calls=%async_computation.2 | async-start | bytes 12582912 | tf_op jit(solution)/shard_map/all_to_all | solution.py:53
  126.1 0.1 reduce
  126.2 0.1 reshape.75
  126.3 140.1 %all-to-all-done.2 = f32[32,192,256]{2,1,0:T(8,128)} async-done(((f32[32,192,256]{2,1,0:T(8,128)}), f32[32,192,256]{2,1,0:T(8,128)}, u32[]{:S(2)}, u32[]{:S(2)}) %all-to-all-start.2) | async-done | bytes 6291488 | tf_op jit(solution)/shard_map/all_to_all | solution.py:53
  266.4 36.2 %scatter_custom_fusion = f32[4008,256]{1,0:T(8,128)} fusion(s32[6144]{0:T(1024)S(1)} %reshape.75, f32[6144,256]{1,0:T(8,128)} %bitcast.10, f32[]{:T(128)} %constant.18.clone.1), kind=kCustom, calls=%fused_computation.4 | custom fusion | flops 1572864 | bytes 4104704 | tf_op jit(solution)/shard_map/scatter-add | solution.py:58
  302.7 3.7 %convert_element_type.7 = bf16[4008,256]{1,0:T(8,128)(2,1)} convert(f32[4008,256]{1,0:T(8,128)} %scatter_custom_fusion) | non-fusion elementwise | flops 1026048 | bytes 6156288 | tf_op jit(solution)/shard_map/convert_element_type | solution.py:59
  (10 shorter events, 0.1 us)
Async XLA Ops:
  0.0 10.4 %copy-start = (s32[128]{0:T(128)S(1)}, s32[128]{0:T(128)}, u32[]{:S(2)}) copy-start(s32[128]{0:T(128)} %param.3) | copy-start | bytes 1540
  3.2 68.1 %all-to-all-start.1 = ((f32[128,16,256]{2,0,1:T(8,128)}), f32[128,16,256]{2,0,1:T(8,128)S(1)}, u32[]{:S(2)}, u32[]{:S(2)}) async-start(f32[128,16,256]{2,0,1:T(8,128)} %bitcast.28), calls=%async_computation.1 | async-start | bytes 4194304 | tf_op jit(solution)/shard_map/all_to_all | solution.py:46
  71.3 45.0 %all-to-all-start = ((s32[32,1,192]{2,1,0:T(1,128)}), s32[32,1,192]{2,1,0:T(1,128)S(1)}, u32[]{:S(2)}, u32[]{:S(2)}) async-start(s32[32,1,192]{2,1,0:T(1,128)} %copy.22), calls=%async_computation | async-start | bytes 65536 | tf_op jit(solution)/shard_map/all_to_all | solution.py:54
  116.3 150.1 %all-to-all-start.2 = ((f32[32,192,256]{2,1,0:T(8,128)}), f32[32,192,256]{2,1,0:T(8,128)}, u32[]{:S(2)}, u32[]{:S(2)}) async-start(f32[32,192,256]{2,1,0:T(8,128)} %select_select_fusion), calls=%async_computation.2 | async-start | bytes 12582912 | tf_op jit(solution)/shard_map/all_to_all | solution.py:53
where the time goes:
time: 307 us; the launch traced here: 306 us
  waiting for transfers between devices  140 us (46%)
  blocking collectives  58.8 us (19%)
  other arithmetic  49.7 us (16%)
  starting transfers between devices  29.6 us (10%)
  local copies, waits for them, and re-layouts  27.9 us (9%)
    all_to_all x1, waiting for transfers between devices, local(): lax.all_to_all(outgoing, 'vocab', split_axis=0, concat_axis=0, tiled=True)  140 us
    all_gather x1, blocking collectives, turned_gather(): whole, at, outs = (lax.all_gather(both, axis, axis=0, tiled=True), 0, [])  58.8 us
    scatter-add x1, other arithmetic, local(): table_sum = jax.ops.segment_sum(columns, row_index, num_segments=rows_own)  36.2 us
    gather x1, local copies, waits for them, and re-layouts, local(): picked = jnp.take(token_cols, index, axis=0)  23.7 us
    all_to_all x1, starting transfers between devices, local(): lax.all_to_all(row_all, 'vocab', split_axis=0, concat_axis=0, tiled=True)  12.6 us
    all_to_all x1, starting transfers between devices, local(): lax.all_to_all(outgoing, 'vocab', split_axis=0, concat_axis=0, tiled=True)  9.84 us
    select_n x1, other arithmetic, local(): outgoing = jnp.where((token_all >= 0)[:, :, None], picked, 0.0)  8.62 us
    all_to_all x1, starting transfers between devices, local(): lax.all_to_all(out_grads, 'dp', split_axis=1, concat_axis=0, tiled=True)  7.21 us
  transfers between devices with their start and end apart: 3, of which 1 were waited for; matrix products, arithmetic and copies ran while one was open for 11% of the time, Pallas kernels for 0%

commit v1 on v0

--- a/solution.py
+++ b/solution.py
@@ -38,12 +38,24 @@
 
 
 def local(out_grads, token_ids):
+
+    def view_the_lanes(along_axis, here_x):
+        return jnp.concatenate(
+            lax.all_to_all(
+                jnp.stack(jnp.split(here_x, lax.psum(1, along_axis), axis=1), axis=0),
+                along_axis,
+                0,
+                0,
+            ),
+            axis=0,
+        )
+
     owners = lax.axis_size("vocab")
     tok_count = token_ids.shape[0]
     rows_own = VOCAB // owners
     capacity = 3 * tok_count // owners
     token_at, row_at = slot_tables(token_ids, rows_own, owners, capacity)
-    token_cols = lax.all_to_all(out_grads, "dp", split_axis=1, concat_axis=0, tiled=True)
+    token_cols = view_the_lanes("dp", out_grads)
     token_all, row_all = turned_gather((token_at, row_at), "dp", (1, 1))
     source = lax.broadcasted_iota(jnp.int32, token_all.shape, 1) // capacity
     index = source * tok_count + jnp.maximum(token_all, 0)

time: 307 us -> 329 us (1.072)
  local copies, waits for them, and re-layouts: 27.9 us -> 49.7 us
    unnamed x4 -> x19, local copies, waits for them, and re-layouts: 0.08 us -> 23.5 us
where the time goes in v1:
time: 329 us; the launch traced here: 328 us
  waiting for transfers between devices  140 us (43%)
  blocking collectives  58.8 us (18%)
  local copies, waits for them, and re-layouts  49.7 us (15%)
  other arithmetic  49.7 us (15%)
  starting transfers between devices  29.8 us (9%)
    all_to_all x1, waiting for transfers between devices, local(): lax.all_to_all(outgoing, 'vocab', split_axis=0, concat_axis=0, tiled=True)  140 us
    all_gather x1, blocking collectives, turned_gather(): whole, at, outs = (lax.all_gather(both, axis, axis=0, tiled=True), 0, [])  58.8 us
    scatter-add x1, other arithmetic, local(): table_sum = jax.ops.segment_sum(columns, row_index, num_segments=rows_own)  36.2 us
    gather x1, local copies, waits for them, and re-layouts, local(): picked = jnp.take(token_cols, index, axis=0)  23.7 us
    unnamed x19, local copies, waits for them, and re-layouts  23.5 us
    all_to_all x1, starting transfers between devices, local(): lax.all_to_all(row_all, 'vocab', split_axis=0, concat_axis=0, tiled=True)  12.6 us
    all_to_all x1, starting transfers between devices, local(): lax.all_to_all(outgoing, 'vocab', split_axis=0, concat_axis=0, tiled=True)  9.83 us
    select_n x1, other arithmetic, local(): outgoing = jnp.where((token_all >= 0)[:, :, None], picked, 0.0)  8.62 us
  transfers between devices with their start and end apart: 3, of which 1 were waited for; matrix products, arithmetic and copies ran while one was open for 11% of the time, Pallas kernels for 0%

profile of v1, /device:TPU:64, one launch (start us, length us, event | category | flops | bytes accessed | tf_op | source)
XLA Modules:
  0.0 328.3 jit_solution(6765984771206687894)
XLA Ops:
  0.0 1.5 bitcast_dynamic-update-slice_fusion.15
  1.6 1.6 bitcast_dynamic-update-slice_fusion.14
  3.1 1.6 bitcast_dynamic-update-slice_fusion.13
  4.7 1.6 bitcast_dynamic-update-slice_fusion.12
  6.2 1.6 bitcast_dynamic-update-slice_fusion.11
  7.8 1.5 bitcast_dynamic-update-slice_fusion.10
  9.4 1.6 bitcast_dynamic-update-slice_fusion.9
  10.9 1.6 bitcast_dynamic-update-slice_fusion.8
  12.5 1.6 bitcast_dynamic-update-slice_fusion.7
  14.1 1.6 bitcast_dynamic-update-slice_fusion.6
  15.6 1.6 bitcast_dynamic-update-slice_fusion.5
  17.2 1.6 bitcast_dynamic-update-slice_fusion.4
  18.7 1.6 bitcast_dynamic-update-slice_fusion.3
  20.3 1.6 bitcast_dynamic-update-slice_fusion.2
  21.9 1.6 bitcast_dynamic-update-slice_fusion.1
  23.4 1.6 bitcast_dynamic-update-slice_fusion
  25.0 0.0 copy-start
  25.0 7.3 %all-to-all-start.1 = ((f32[16,128,256]{2,1,0:T(8,128)}), f32[16,128,256]{2,1,0:T(8,128)S(1)}, u32[]{:S(2)}, u32[]{:S(2)}) async-start(f32[16,128,256]{2,1,0:T(8,128)} %bitcast_dynamic-update-slice_fusion), calls=%async_computation.1 | async-start | bytes 4194304 | tf_op jit(solution)/shard_map/all_to_all | solution.py:44
  32.3 0.0 copy-done
  32.4 0.2 convert_reduce_fusion
  32.6 0.3 and_reduce_fusion
  32.9 0.5 fusion.2
  33.4 0.1 add_bitcast_fusion
  33.4 58.8 %all-gather = s32[16,12,64]{2,1,0:T(8,128)S(1)} all-gather(s32[1,12,64]{2,1,0:T(8,128)S(1)} %add_bitcast_fusion), channel_id=1, replica_groups=mesh['vocab'=32,'dp'=16] {'dp'}, dimensions={0}, use_global_device_ids=true | all-gather | bytes 52224 | tf_op jit(solution)/shard_map/all_gather | solution.py:12
  92.2 0.1 fusion.5
  92.3 0.1 copy.19
  92.4 0.1 reshape.68
  92.5 0.7 copy.17
  93.2 0.0 all-to-all-done.1
  93.2 12.6 %all-to-all-start = ((s32[32,1,192]{2,1,0:T(1,128)}), s32[32,1,192]{2,1,0:T(1,128)S(1)}, u32[]{:S(2)}, u32[]{:S(2)}) async-start(s32[32,1,192]{2,1,0:T(1,128)} %copy.17), calls=%async_computation | async-start | bytes 65536 | tf_op jit(solution)/shard_map/all_to_all | solution.py:66
  105.8 23.7 %gather_fusion = f32[6144,256]{1,0:T(8,128)} fusion(f32[2048,256]{1,0:T(8,128)S(1)} %bitcast.52, s32[6144]{0:T(1024)S(1)} %broadcast_clamp_fusion), kind=kCustom, calls=%fused_computation | custom fusion | bytes 12607488 | tf_op jit(solution)/shard_map/jit(_take)/gather | solution.py:62
  129.6 8.6 %select_select_fusion = f32[32,192,256]{2,1,0:T(8,128)} fusion(f32[32,192,256]{2,1,0:T(8,128)} %bitcast.53, pred[32,192]{1,0:T(8,128)(4,1)S(1)} %get-tuple-element.7, pred[32,192]{1,0:T(8,128)(4,1)S(1)} %compare_bitcast_fusion), kind=kLoop, calls=%fused_computation.2 | loop fusion | flops 3145728 | bytes 12595200 | tf_op jit(solution)/shard_map/jit(_where)/select_n | solution.py:63
  138.2 0.0 all-to-all-done
  138.2 9.8 %all-to-all-start.2 = ((f32[32,192,256]{2,1,0:T(8,128)}), f32[32,192,256]{2,1,0:T(8,128)}, u32[]{:S(2)}, u32[]{:S(2)}) async-start(f32[32,192,256]{2,1,0:T(8,128)} %select_select_fusion), calls=%async_computation.2 | async-start | bytes 12582912 | tf_op jit(solution)/shard_map/all_to_all | solution.py:65
  148.1 0.1 reduce
  148.1 0.1 reshape.76
  148.2 140.1 %all-to-all-done.2 = f32[32,192,256]{2,1,0:T(8,128)} async-done(((f32[32,192,256]{2,1,0:T(8,128)}), f32[32,192,256]{2,1,0:T(8,128)}, u32[]{:S(2)}, u32[]{:S(2)}) %all-to-all-start.2) | async-done | bytes 6291488 | tf_op jit(solution)/shard_map/all_to_all | solution.py:65
  288.4 36.2 %scatter_custom_fusion = f32[4008,256]{1,0:T(8,128)} fusion(s32[6144]{0:T(1024)S(1)} %reshape.76, f32[6144,256]{1,0:T(8,128)} %bitcast.25, f32[]{:T(128)} %constant.18.clone.1), kind=kCustom, calls=%fused_computation.3 | custom fusion | flops 1572864 | bytes 4104704 | tf_op jit(solution)/shard_map/scatter-add | solution.py:70
  324.6 3.7 %convert_element_type.7 = bf16[4008,256]{1,0:T(8,128)(2,1)} convert(f32[4008,256]{1,0:T(8,128)} %scatter_custom_fusion) | non-fusion elementwise | flops 1026048 | bytes 6156288 | tf_op jit(solution)/shard_map/convert_element_type | solution.py:71
  (10 shorter events, 0.1 us)
Async XLA Ops:
  25.0 7.3 %copy-start = (s32[128]{0:T(128)S(1)}, s32[128]{0:T(128)}, u32[]{:S(2)}) copy-start(s32[128]{0:T(128)} %param.3) | copy-start | bytes 1540
  25.0 68.3 %all-to-all-start.1 = ((f32[16,128,256]{2,1,0:T(8,128)}), f32[16,128,256]{2,1,0:T(8,128)S(1)}, u32[]{:S(2)}, u32[]{:S(2)}) async-start(f32[16,128,256]{2,1,0:T(8,128)} %bitcast_dynamic-update-slice_fusion), calls=%async_computation.1 | async-start | bytes 4194304 | tf_op jit(solution)/shard_map/all_to_all | solution.py:44
  93.2 45.0 %all-to-all-start = ((s32[32,1,192]{2,1,0:T(1,128)}), s32[32,1,192]{2,1,0:T(1,128)S(1)}, u32[]{:S(2)}, u32[]{:S(2)}) async-start(s32[32,1,192]{2,1,0:T(1,128)} %copy.17), calls=%async_computation | async-start | bytes 65536 | tf_op jit(solution)/shard_map/all_to_all | solution.py:66
  138.2 150.1 %all-to-all-start.2 = ((f32[32,192,256]{2,1,0:T(8,128)}), f32[32,192,256]{2,1,0:T(8,128)}, u32[]{:S(2)}, u32[]{:S(2)}) async-start(f32[32,192,256]{2,1,0:T(8,128)} %select_select_fusion), calls=%async_computation.2 | async-start | bytes 12582912 | tf_op jit(solution)/shard_map/all_to_all | solution.py:65

commit v2 on v0

--- a/solution.py
+++ b/solution.py
@@ -2,6 +2,7 @@
 import jax.numpy as jnp
 from jax import lax
 from jax.sharding import PartitionSpec as P
+from jax.lax import all_to_all, axis_size
 
 VOCAB = 128256
 
@@ -9,7 +10,10 @@
 def turned_gather(arrays, axis, dims):
     turned = [jnp.moveaxis(a, dim, 0) for a, dim in zip(arrays, dims)]
     both = jnp.concatenate([t.reshape(len(t), -1) for t in turned], axis=1)
-    whole, at, outs = (lax.all_gather(both, axis, axis=0, tiled=True), 0, [])
+    _manage_sites = lambda in_array, shard_axis: jnp.concatenate(
+        all_to_all(jnp.stack(axis_size(shard_axis) * [in_array]), shard_axis, 0, 0), axis=0
+    )
+    whole, at, outs = (_manage_sites(both, axis), 0, [])
     for t, dim in zip(turned, dims):
         share = whole[:, at : at + t[0].size].reshape(-1, *t.shape[1:])
         outs.append(jnp.moveaxis(share, 0, dim))

time: 307 us -> 306 us (level)
  blocking collectives: 58.8 us -> 0 us
  waiting for transfers between devices: 140 us -> 192 us
  starting transfers between devices: 29.6 us -> 33.3 us
    all_gather x1 -> x0, blocking collectives: 58.8 us -> none  [turned_gather(): whole, at, outs = (lax.all_gather(both, axis, axis=0, tiled=True), 0, [])]
    all_to_all x1, waiting for transfers between devices: 0.01 us -> 46.8 us  [local(): lax.all_to_all(out_grads, 'dp', split_axis=1, concat_axis=0, tiled=True)]
    all_to_all x0 -> x1, starting transfers between devices: none -> 7.21 us  [turned_gather(): all_to_all(jnp.stack(axis_size(shard_axis) * [in_array]), shard_axis, 0, 0)]
    all_to_all x0 -> x1, waiting for transfers between devices: none -> 4.57 us  [turned_gather(): all_to_all(jnp.stack(axis_size(shard_axis) * [in_array]), shard_axis, 0, 0)]
    all_to_all x1, starting transfers between devices: 7.21 us -> 3.72 us  [local(): lax.all_to_all(out_grads, 'dp', split_axis=1, concat_axis=0, tiled=True)]
  transfers between devices with their start and end apart: 3 -> 4, of which waited for: 1 -> 3; matrix products, arithmetic and copies ran while one was open for 11% -> 12% of each run, Pallas kernels for 0% -> 0%
where the time goes in v2:
time: 306 us; the launch traced here: 305 us
  waiting for transfers between devices  192 us (63%)
  other arithmetic  51.1 us (17%)
  starting transfers between devices  33.3 us (11%)
  local copies, waits for them, and re-layouts  29.3 us (10%)
    all_to_all x1, waiting for transfers between devices, local(): lax.all_to_all(outgoing, 'vocab', split_axis=0, concat_axis=0, tiled=True)  140 us
    all_to_all x1, waiting for transfers between devices, local(): lax.all_to_all(out_grads, 'dp', split_axis=1, concat_axis=0, tiled=True)  46.8 us
    scatter-add x1, other arithmetic, local(): table_sum = jax.ops.segment_sum(columns, row_index, num_segments=rows_own)  36.2 us
    gather x1, local copies, waits for them, and re-layouts, local(): picked = jnp.take(token_cols, index, axis=0)  23.7 us
    all_to_all x1, starting transfers between devices, local(): lax.all_to_all(row_all, 'vocab', split_axis=0, concat_axis=0, tiled=True)  12.6 us
    all_to_all x1, starting transfers between devices, local(): lax.all_to_all(outgoing, 'vocab', split_axis=0, concat_axis=0, tiled=True)  9.83 us
    select_n x1, other arithmetic, local(): outgoing = jnp.where((token_all >= 0)[:, :, None], picked, 0.0)  8.62 us
    all_to_all x1, starting transfers between devices, turned_gather(): all_to_all(jnp.stack(axis_size(shard_axis) * [in_array]), shard_axis, 0, 0)  7.21 us
  transfers between devices with their start and end apart: 4, of which 3 were waited for; matrix products, arithmetic and copies ran while one was open for 12% of the time, Pallas kernels for 0%

profile of v2, /device:TPU:64, one launch (start us, length us, event | category | flops | bytes accessed | tf_op | source)
XLA Modules:
  0.0 305.4 jit_solution(8045604549020845272)
XLA Ops:
  0.0 0.7 multiply_subtract_fusion
  0.7 0.2 convert_reduce_fusion
  0.9 0.3 and_reduce_fusion
  1.2 0.5 fusion.2
  1.7 0.1 pad_add_fusion
  1.8 0.7 reshape.93
  2.5 7.2 %all-to-all-start = ((s32[16,1,768]{2,1,0:T(1,128)}), s32[16,1,768]{2,1,0:T(1,128)S(1)}, u32[]{:S(2)}, u32[]{:S(2)}) async-start(s32[16,1,768]{2,1,0:T(1,128)} %reshape.93), calls=%async_computation | async-start | bytes 98304 | tf_op jit(solution)/shard_map/all_to_all | solution.py:14
  9.7 3.2 %copy.28 = f32[16,16,8,256]{3,2,0,1:T(8,128)} copy(f32[16,16,8,256]{3,2,1,0:T(8,128)} %bitcast.27) | data formatting | bytes 4194304 | tf_op jit(solution)/shard_map/all_to_all | solution.py:50
  12.9 4.6 %all-to-all-done = s32[16,1,768]{2,1,0:T(1,128)S(1)} async-done(((s32[16,1,768]{2,1,0:T(1,128)}), s32[16,1,768]{2,1,0:T(1,128)S(1)}, u32[]{:S(2)}, u32[]{:S(2)}) %all-to-all-start) | async-done | bytes 49184 | tf_op jit(solution)/shard_map/all_to_all | solution.py:14
  17.4 3.7 %all-to-all-start.2 = ((f32[128,16,256]{2,0,1:T(8,128)}), f32[128,16,256]{2,0,1:T(8,128)S(1)}, u32[]{:S(2)}, u32[]{:S(2)}) async-start(f32[128,16,256]{2,0,1:T(8,128)} %bitcast.26), calls=%async_computation.2 | async-start | bytes 4194304 | tf_op jit(solution)/shard_map/all_to_all | solution.py:50
  21.2 0.5 broadcast.86
  21.7 0.8 reduce.1
  22.5 0.1 reshape.94
  22.6 0.1 fusion.5
  22.7 0.1 copy.25
  22.8 0.1 reshape.73
  22.9 0.7 copy.22
  23.6 46.8 %all-to-all-done.2 = f32[128,16,256]{2,0,1:T(8,128)S(1)} async-done(((f32[128,16,256]{2,0,1:T(8,128)}), f32[128,16,256]{2,0,1:T(8,128)S(1)}, u32[]{:S(2)}, u32[]{:S(2)}) %all-to-all-start.2) | async-done | bytes 2097184 | tf_op jit(solution)/shard_map/all_to_all | solution.py:50
  70.3 12.6 %all-to-all-start.1 = ((s32[32,1,192]{2,1,0:T(1,128)}), s32[32,1,192]{2,1,0:T(1,128)S(1)}, u32[]{:S(2)}, u32[]{:S(2)}) async-start(s32[32,1,192]{2,1,0:T(1,128)} %copy.22), calls=%async_computation.1 | async-start | bytes 65536 | tf_op jit(solution)/shard_map/all_to_all | solution.py:58
  82.9 23.7 %gather_fusion = f32[6144,256]{1,0:T(8,128)} fusion(f32[2048,256]{1,0:T(8,128)S(1)} %bitcast.24, s32[6144]{0:T(1024)S(1)} %broadcast_clamp_fusion), kind=kCustom, calls=%fused_computation | custom fusion | bytes 12607488 | tf_op jit(solution)/shard_map/jit(_take)/gather | solution.py:54
  106.7 8.6 %select_select_fusion = f32[32,192,256]{2,1,0:T(8,128)} fusion(f32[32,192,256]{2,1,0:T(8,128)} %bitcast.25, pred[32,192]{1,0:T(8,128)(4,1)S(1)} %get-tuple-element.7, pred[32,192]{1,0:T(8,128)(4,1)S(1)} %compare_bitcast_fusion), kind=kLoop, calls=%fused_computation.2 | loop fusion | flops 3145728 | bytes 12595200 | tf_op jit(solution)/shard_map/jit(_where)/select_n | solution.py:55
  115.3 0.0 all-to-all-done.1
  115.3 9.8 %all-to-all-start.3 = ((f32[32,192,256]{2,1,0:T(8,128)}), f32[32,192,256]{2,1,0:T(8,128)}, u32[]{:S(2)}, u32[]{:S(2)}) async-start(f32[32,192,256]{2,1,0:T(8,128)} %select_select_fusion), calls=%async_computation.3 | async-start | bytes 12582912 | tf_op jit(solution)/shard_map/all_to_all | solution.py:57
  125.1 0.1 reduce
  125.2 0.1 reshape.81
  125.3 140.2 %all-to-all-done.3 = f32[32,192,256]{2,1,0:T(8,128)} async-done(((f32[32,192,256]{2,1,0:T(8,128)}), f32[32,192,256]{2,1,0:T(8,128)}, u32[]{:S(2)}, u32[]{:S(2)}) %all-to-all-start.3) | async-done | bytes 6291488 | tf_op jit(solution)/shard_map/all_to_all | solution.py:57
  265.5 36.2 %scatter_custom_fusion = f32[4008,256]{1,0:T(8,128)} fusion(s32[6144]{0:T(1024)S(1)} %reshape.81, f32[6144,256]{1,0:T(8,128)} %bitcast.9, f32[]{:T(128)} %constant.18.clone.1), kind=kCustom, calls=%fused_computation.4 | custom fusion | flops 1572864 | bytes 4104704 | tf_op jit(solution)/shard_map/scatter-add | solution.py:62
  301.8 3.7 %convert_element_type.7 = bf16[4008,256]{1,0:T(8,128)(2,1)} convert(f32[4008,256]{1,0:T(8,128)} %scatter_custom_fusion) | non-fusion elementwise | flops 1026048 | bytes 6156288 | tf_op jit(solution)/shard_map/convert_element_type | solution.py:63
  (10 shorter events, 0.1 us)
Async XLA Ops:
  2.5 15.0 %all-to-all-start = ((s32[16,1,768]{2,1,0:T(1,128)}), s32[16,1,768]{2,1,0:T(1,128)S(1)}, u32[]{:S(2)}, u32[]{:S(2)}) async-start(s32[16,1,768]{2,1,0:T(1,128)} %reshape.93), calls=%async_computation | async-start | bytes 98304 | tf_op jit(solution)/shard_map/all_to_all | solution.py:14
  17.4 52.9 %all-to-all-start.2 = ((f32[128,16,256]{2,0,1:T(8,128)}), f32[128,16,256]{2,0,1:T(8,128)S(1)}, u32[]{:S(2)}, u32[]{:S(2)}) async-start(f32[128,16,256]{2,0,1:T(8,128)} %bitcast.26), calls=%async_computation.2 | async-start | bytes 4194304 | tf_op jit(solution)/shard_map/all_to_all | solution.py:50
  70.3 45.0 %all-to-all-start.1 = ((s32[32,1,192]{2,1,0:T(1,128)}), s32[32,1,192]{2,1,0:T(1,128)S(1)}, u32[]{:S(2)}, u32[]{:S(2)}) async-start(s32[32,1,192]{2,1,0:T(1,128)} %copy.22), calls=%async_computation.1 | async-start | bytes 65536 | tf_op jit(solution)/shard_map/all_to_all | solution.py:58
  115.3 150.3 %all-to-all-start.3 = ((f32[32,192,256]{2,1,0:T(8,128)}), f32[32,192,256]{2,1,0:T(8,128)}, u32[]{:S(2)}, u32[]{:S(2)}) async-start(f32[32,192,256]{2,1,0:T(8,128)} %select_select_fusion), calls=%async_computation.3 | async-start | bytes 12582912 | tf_op jit(solution)/shard_map/all_to_all | solution.py:57
